TPU v7x, 32 devices: a whole 2x2x4 slice. The times are simulated.
32 devices in a mesh: grp: 2 (over y), dp: 4 (over z), mp: 4 (over x, core).
Axes of the slice: x: 2, y: 2, z: 4, core: 2. Of those that a mesh axis runs over, the one named last changes fastest.
Arguments:
- tokens: bfloat16 [12288, 4096], P(('grp', 'dp'), 'mp'), parts along dimension 0, may hold values from -6 to 6
- out_grad: bfloat16 [12288, 11008], P(('grp', 'dp'), 'mp'), parts along dimension 0, may hold values from -0.109375 to 0.109375
- subspace_basis: bfloat16 [4096, 512], P('mp'), may hold values from -0.09375 to 0.09375
- weights: bfloat16 [4, 2752, 4096], P('mp', 'dp'), may hold values from -0.09375 to 0.09375
- moment_first: float32 [4, 5504, 512], P('mp', ('grp', 'dp')), parts along dimension 1, may hold values from -6 to 6
- moment_second: float32 [4, 5504, 512], P('mp', ('grp', 'dp')), parts along dimension 1, may hold values from 0.01 to 2
Outputs:
- new_weights: bfloat16 [4, 5504, 4096], P(None, ('grp', 'dp')), parts along dimension 1
- first_moment: float32 [4, 5504, 512], P('mp', ('grp', 'dp')), parts along dimension 1
- second_moment: float32 [4, 5504, 512], P('mp', ('grp', 'dp')), parts along dimension 1
There are 2 independent parts, one for each index of `grp`. A program takes and returns all parts, laid end to end along the dimension named above; an argument that names none is the same for every part. Nothing has to cross between parts.
All inputs are finite; a program needn't handle non-finite values.
Results may differ from a plain program's by a relative error of at most 0.004.
Values may be sent and summed in bfloat16 or wider, within the bound.
A program may use at most 192 MiB of HBM per device.

v0:
```python
import jax
import jax.numpy as jnp
from jax import lax
from jax.sharding import PartitionSpec as P

beta_one = 0.9
beta_two = 0.999
correction_one = 1.0 - 0.9**10
correction_two = 1.0 - 0.999**10
epsilon = 1e-08
step_size = 0.02


def shards(tokens, out_grad, subspace_basis, weights, moment_first, moment_second):
    partial_value = jnp.dot(tokens, subspace_basis, preferred_element_type=jnp.float32)
    projected = lax.psum(partial_value.astype(jnp.bfloat16), "mp")
    subspace = lax.psum_scatter(
        lax.dot_general(
            out_grad, projected, (((0,), (0,)), ((), ())), preferred_element_type=jnp.float32
        ).astype(jnp.bfloat16),
        "dp",
        scatter_dimension=0,
        tiled=True,
    ).astype(jnp.float32)
    gradient = subspace[None]
    first_new = beta_one * moment_first + (1.0 - beta_one) * gradient
    second_new = beta_two * moment_second + (1.0 - beta_two) * gradient * gradient
    direction = (
        first_new / correction_one / (jnp.sqrt(second_new / correction_two) + epsilon)
    ).astype(jnp.bfloat16)
    weight_delta = lax.dot_general(
        direction[0],
        lax.all_gather(subspace_basis, "mp", axis=0, tiled=True),
        (((1,), (1,)), ((), ())),
        preferred_element_type=jnp.float32,
    )
    updated = (weights[0].astype(jnp.float32) - step_size * weight_delta).astype(jnp.bfloat16)
    result = lax.all_gather(updated[None], "mp", axis=0, tiled=True)
    return (result, first_new, second_new)


def solution(mesh):
    return jax.shard_map(
        shards,
        mesh=mesh,
        in_specs=(
            P(("grp", "dp"), "mp"),
            P(("grp", "dp"), "mp"),
            P("mp", None),
            P("mp", "dp", None),
            P("mp", ("grp", "dp"), None),
            P("mp", ("grp", "dp"), None),
        ),
        out_specs=(
            P(None, ("grp", "dp"), None),
            P("mp", ("grp", "dp"), None),
            P("mp", ("grp", "dp"), None),
        ),
        check_vma=False,
    )
```

profile of v0, /device:TPU:0, one launch (start us, length us, event | category | flops | bytes accessed | tf_op | source)
XLA Modules:
  0.0 337.7 jit_solution(18410038620376296713)
XLA Ops:
  7.2 0.0 copy-start
  7.2 0.0 all-reduce.2.cloned.1.call-start
  7.2 1.8 copy-done
  9.1 4.2 %convolution_convert_fusion.1 = bf16[1536,512]{1,0:T(8,128)(2,1)} fusion(bf16[1536,1024]{1,0:T(8,128)(2,1)S(1)} %copy-done, bf16[1024,512]{1,0:T(8,128)(2,1)} %param.8), kind=kOutput, calls=%fused_computation.4 | convolution fusion | flops 1611399168 | bytes 5767168 | tf_op jit(solution)/shard_map/dot_general | solution.py:15
  13.2 0.0 all-reduce.2.cloned.1.call-update
  13.3 0.0 reduce-scatter.2.cloned.1.call-start
  13.3 45.6 %all-reduce.2.cloned.1.call-done = bf16[1536,512]{1,0:T(8,128)(2,1)} async-done(((bf16[1536,512]{1,0:T(8,128)(2,1)}), bf16[1536,512]{1,0:T(8,128)(2,1)}) %all-reduce.2.cloned.1.call-update) | async-done | bytes 1572880 | tf_op jit(solution)/shard_map/psum | solution.py:16
  59.0 9.9 %fusion.1 = bf16[2752,512]{1,0:T(8,128)(2,1)} fusion(bf16[1536,2752]{0,1:T(8,128)(2,1)} %param.7, bf16[1536,512]{1,0:T(8,128)(2,1)} %all-reduce.2.cloned.1.call-done), kind=kOutput, calls=%fused_computation.3 | convolution fusion | flops 4329930752 | bytes 12845056 | tf_op jit(solution)/shard_map/dot_general | solution.py:18
  68.9 0.0 copy-start.2
  68.9 0.0 copy-start.3
  68.9 0.0 reduce-scatter.2.cloned.1.call-update
  68.9 0.0 all-gather.4.cloned.1.call-start
  69.0 0.7 all-gather.4.cloned.1.call-update
  69.6 0.0 all-gather.6.cloned.1.call-start
  69.7 54.6 %reduce-scatter.2.cloned.1.call-done = bf16[688,512]{1,0:T(8,128)(2,1)} async-done(((bf16[2752,512]{1,0:T(8,128)(2,1)}), bf16[688,512]{1,0:T(8,128)(2,1)}) %reduce-scatter.2.cloned.1.call-update) | async-done | bytes 704528 | tf_op jit(solution)/shard_map/reduce_scatter | solution.py:17
  124.3 0.0 copy-done.2
  124.3 0.0 copy-done.3
  124.3 3.2 fusion.3
  127.5 32.8 %all-gather.4.cloned.1.call-done = bf16[4096,512]{1,0:T(8,128)(2,1)} async-done(((bf16[1024,512]{1,0:T(8,128)(2,1)}), bf16[4096,512]{1,0:T(8,128)(2,1)}) %all-gather.4.cloned.1.call-update) | async-done | bytes 4194320 | tf_op jit(solution)/shard_map/all_gather | solution.py:33
  160.2 10.7 %fusion = bf16[688,4096]{1,0:T(8,128)(2,1)} fusion(bf16[4096,512]{1,0:T(8,128)(2,1)} %all-gather.4.cloned.1.call-done, bf16[1,688,4096]{2,1,0:T(8,128)(2,1)} %param.9, f32[1,688,512]{2,1,0:T(8,128)} %get-tuple-element.10, f32[1,688,512]{2,1,0:T(8,128)} %get-tuple-element.9), kind=kOutput, calls=%fused_computation.1 | convolution fusion | flops 2898714624 | bytes 18284544 | tf_op jit(solution)/shard_map/dot_general | solution.py:31
  170.9 0.0 all-gather.6.cloned.1.call-update
  170.9 140.5 %all-gather.6.cloned.1.call-done = bf16[2752,4096]{1,0:T(8,128)(2,1)} async-done(((bf16[688,4096]{1,0:T(8,128)(2,1)}), bf16[2752,4096]{1,0:T(8,128)(2,1)}) %all-gather.6.cloned.1.call-update) | async-done | bytes 22544400 | tf_op jit(solution)/shard_map/all_gather | solution.py:38
  311.4 0.0 copy-start.1
  311.4 19.8 %copy.11 = bf16[4,688,4096]{2,1,0:T(8,128)(2,1)} copy(bf16[4,688,4096]{2,1,0:T(8,128)(2,1)} %bitcast.22) | data formatting | bytes 45088768
  331.2 0.0 copy-done.1
Async XLA Ops:
  7.2 1.9 copy-start
  7.2 51.8 %all-reduce.2.cloned.1.call-start = ((), (), s32[]{:S(2)}) async-start(), calls=%async_computation.1 | async-start | bytes 3145728 | tf_op jit(solution)/shard_map/psum | solution.py:16
  13.3 111.0 %reduce-scatter.2.cloned.1.call-start = ((), (), s32[]{:S(2)}) async-start(), calls=%async_computation.2 | async-start | bytes 3522560 | tf_op jit(solution)/shard_map/reduce_scatter | solution.py:17
  68.9 55.4 %copy-start.2 = (f32[1,688,512]{2,1,0:T(8,128)S(1)}, f32[1,688,512]{2,1,0:T(8,128)}, u32[]{:S(2)}) copy-start(f32[1,688,512]{2,1,0:T(8,128)} %param.10) | copy-start | bytes 4227076
  68.9 55.4 %copy-start.3 = (f32[1,688,512]{2,1,0:T(8,128)S(1)}, f32[1,688,512]{2,1,0:T(8,128)}, u32[]{:S(2)}) copy-start(f32[1,688,512]{2,1,0:T(8,128)} %param.11) | copy-start | bytes 4227076
  68.9 91.3 %all-gather.4.cloned.1.call-start = ((), (), s32[]{:S(2)}) async-start(), calls=%async_computation.3 | async-start | bytes 5242880 | tf_op jit(solution)/shard_map/all_gather | solution.py:33
  69.6 241.7 %all-gather.6.cloned.1.call-start = ((), (), s32[]{:S(2)}) async-start(), calls=%async_computation.4 | async-start | bytes 28180480 | tf_op jit(solution)/shard_map/all_gather | solution.py:38
  311.4 19.8 %copy-start.1 = (bf16[1536,1024]{1,0:T(8,128)(2,1)S(1)}, bf16[1536,1024]{1,0:T(8,128)(2,1)}, u32[]{:S(2)}) copy-start(bf16[1536,1024]{1,0:T(8,128)(2,1)} %param.6) | copy-start | bytes 9437188
Sparse Core Ops, SparseCore 0:
  13.4 45.5 all-reduce.1
  69.0 55.2 reduce-scatter.1
  125.9 34.2 all-gather.3
  171.0 140.3 all-gather.5
where the time goes:
time: 338 us
  waiting for transfers between devices  274 us (81%)
  matrix products  24.7 us (7%)
  local copies, waits for them, and re-layouts  21.6 us (6%)
  between operations  13.8 us (4%)
    all_gather x1, waiting for transfers between devices, shards(): result = lax.all_gather(updated[None], 'mp', axis=0, tiled=True)  140 us
    reduce_scatter x1, waiting for transfers between devices, shards(): lax.psum_scatter(lax.dot_general(out_grad, projected, (((0,), (0,)), ((),...  54.6 us
    psum x1, waiting for transfers between devices, shards(): projected = lax.psum(partial_value.astype(jnp.bfloat16), 'mp')  45.6 us
    all_gather x1, waiting for transfers between devices, shards(): lax.all_gather(subspace_basis, 'mp', axis=0, tiled=True)  32.8 us
    unnamed x9, local copies, waits for them, and re-layouts  21.6 us
    dot_general x1, matrix products, shards(): lax.dot_general(direction[0], lax.all_gather(subspace_basis, 'mp', axis=0...  10.7 us
    dot_general x1, matrix products, shards(): lax.dot_general(out_grad, projected, (((0,), (0,)), ((), ())), preferred_...  9.92 us
  transfers between devices with their start and end apart: 4, of which 4 were waited for; matrix products, arithmetic and copies ran while one was open for 1% of the time, Pallas kernels for 0%

commit v1 on v0

--- a/solution.py
+++ b/solution.py
@@ -1,6 +1,10 @@
+import functools
+
 import jax
 import jax.numpy as jnp
 from jax import lax
+from jax.experimental import pallas as pl
+from jax.experimental.pallas import tpu as pltpu
 from jax.sharding import PartitionSpec as P
 
 beta_one = 0.9
@@ -9,6 +13,364 @@
 correction_two = 1.0 - 0.999**10
 epsilon = 1e-08
 step_size = 0.02
+
+MESH = pl.DeviceIdType.MESH
+bf16 = jnp.bfloat16
+f32 = jnp.float32
+
+RC = 2
+WC = 8
+
+
+def exchange_kernel(
+    n_dp,
+    tokens, out_grad, basis, weights, moment_one, moment_two,
+    first_out, second_out, dirs, bases, walls,
+    tok_v, bas_v, og_v, p_own, p_send, p_recv, s_send, s_recv, proj,
+    g_send, g_recv, m_one, m_two, direction,
+    load_sem, store_sem,
+    pc_s, pc_r, px_s, px_r, pf_s, pf_r, rs_s, rs_r,
+    dc_s, dc_r, dx_s, dx_r, df_s, df_r,
+    bc_s, bc_r, bx_s, bx_r, by_s, by_r, bf_s, bf_r, bg_s, bg_r,
+    wc_s, wc_r, wx_s, wx_r, wy_s, wy_r, wf_s, wf_r, wg_s, wg_r,
+):
+    grp = lax.axis_index("grp")
+    dp = lax.axis_index("dp")
+    mp = lax.axis_index("mp")
+    core = mp % 2
+    mate = mp + 1 - 2 * core
+    across = mp + 2 - 4 * (mp // 2)
+    to_core = {"mp": mate}
+    to_x = {"mp": across}
+    to_y = {"grp": 1 - grp}
+
+    tokens_own, depth = tokens.shape
+    half = tokens_own // 2
+    rank = basis.shape[1]
+    rc = rank // RC
+    hidden = weights.shape[1]
+    wide = weights.shape[2]
+    wh = wide // 2
+    wc = wh // WC
+    bh = depth // 2
+
+    def remote(src, dst, ss, rs, where):
+        return pltpu.make_async_remote_copy(
+            src_ref=src, dst_ref=dst, send_sem=ss, recv_sem=rs,
+            device_id=where, device_id_type=MESH,
+        )
+
+    loads = [
+        pltpu.make_async_copy(src, dst, load_sem.at[i])
+        for i, (src, dst) in enumerate(
+            [(tokens, tok_v), (basis, bas_v), (out_grad, og_v),
+             (moment_one, m_one), (moment_two, m_two)]
+        )
+    ]
+    loads[1].start()
+    loads[0].start()
+    loads[2].start()
+
+    barrier = pltpu.get_barrier_semaphore()
+    for where in (to_core, to_x, to_y):
+        pl.semaphore_signal(barrier, inc=1, device_id=where, device_id_type=MESH)
+    for d in range(1, n_dp):
+        pl.semaphore_signal(
+            barrier, inc=1, device_id={"dp": (dp + d) % n_dp}, device_id_type=MESH
+        )
+    pl.semaphore_wait(barrier, 3 + n_dp - 1)
+
+    def w_cols(side, k):
+        return pl.ds(side * wh + k * wc, wc)
+
+    def w_x(k):
+        return remote(weights.at[0, :, w_cols(grp, k)], walls.at[mp, :, w_cols(grp, k)],
+                      wx_s.at[k], wx_r.at[k], to_x)
+
+    def w_y(k):
+        view = walls.at[across, :, w_cols(grp, k)]
+        return remote(view, view, wy_s.at[k], wy_r.at[k], to_y)
+
+    def w_f(k):
+        view = walls.at[across, :, w_cols(grp, k)]
+        return remote(view, view, wf_s.at[k], wf_r.at[k], to_core)
+
+    def w_g(k):
+        view = walls.at[across, :, w_cols(1 - grp, k)]
+        return remote(view, view, wg_s.at[k], wg_r.at[k], to_core)
+
+    w_x(0).start()
+
+    def project(r, row, dst):
+        def body(i, _):
+            at = pl.multiple_of(row + i * 256, 256)
+            dst[pl.ds(pl.multiple_of(i * 256, 256), 256), :] = jnp.dot(
+                tok_v[pl.ds(at, 256), :], bas_v[:, r * rc:(r + 1) * rc],
+                preferred_element_type=f32,
+            ).astype(dst.dtype)
+            return 0
+        lax.fori_loop(0, half // 256, body, 0)
+
+    def pc(r):
+        return remote(p_send.at[r], p_recv.at[r], pc_s.at[r], pc_r.at[r], to_core)
+
+    def px(r):
+        return remote(s_send.at[r], s_recv.at[r], px_s.at[r], px_r.at[r], to_x)
+
+    def pf(r):
+        view = proj.at[r, pl.ds(core * half, half), :]
+        return remote(view, view, pf_s.at[r], pf_r.at[r], to_core)
+
+    loads[1].wait()
+    loads[0].wait()
+    for r in range(RC):
+        project(r, (1 - core) * half, p_send.at[r])
+        pc(r).start()
+        project(r, core * half, p_own)
+        pc(r).wait_recv()
+        s_send[r] = (p_own[...] + p_recv[r].astype(f32)).astype(bf16)
+        px(r).start()
+
+    loads[3].start()
+    loads[4].start()
+
+    own_w = pltpu.make_async_copy(weights.at[0], walls.at[mp], store_sem.at[2])
+    own_w.start()
+    w_core = remote(weights.at[0], walls.at[mp], wc_s.at[0], wc_r.at[0], to_core)
+    w_core.start()
+    own_b = pltpu.make_async_copy(basis, bases.at[mp], store_sem.at[3])
+    own_b.start()
+    b_core = remote(basis, bases.at[mp], bc_s.at[0], bc_r.at[0], to_core)
+    b_core.start()
+    rows_mine = pl.ds(grp * bh, bh)
+    rows_other = pl.ds((1 - grp) * bh, bh)
+    b_x = remote(basis.at[rows_mine, :], bases.at[mp, rows_mine, :], bx_s.at[0], bx_r.at[0], to_x)
+    b_view = bases.at[across, rows_mine, :]
+    b_y = remote(b_view, b_view, by_s.at[0], by_r.at[0], to_y)
+    b_f = remote(b_view, b_view, bf_s.at[0], bf_r.at[0], to_core)
+    b_view_other = bases.at[across, rows_other, :]
+    b_g = remote(b_view_other, b_view_other, bg_s.at[0], bg_r.at[0], to_core)
+
+    def rs(r, d):
+        to = (dp + d) % n_dp
+        return remote(g_send.at[r, pl.ds(to * hidden, hidden), :], g_recv.at[d - 1, r],
+                      rs_s.at[r, d - 1], rs_r.at[r, d - 1], {"dp": to})
+
+    width = out_grad.shape[1]
+    tile = 256
+    full = width // tile
+
+    def gradient(r, at, size):
+        g_send[r, pl.ds(at, size), :] = lax.dot_general(
+            og_v[:, pl.ds(at, size)], proj[r], (((0,), (0,)), ((), ())),
+            preferred_element_type=f32,
+        ).astype(bf16)
+
+    for r in range(RC):
+        px(r).wait_recv()
+        if r == RC - 1:
+            for k in range(1, WC):
+                w_x(k).start()
+            b_x.start()
+        proj[r, pl.ds(core * half, half), :] = (
+            s_send[r].astype(f32) + s_recv[r].astype(f32)
+        ).astype(bf16)
+        pf(r).start()
+        if r == 0:
+            loads[2].wait()
+        pf(r).wait_recv()
+
+        def body(i, _, r=r):
+            gradient(r, pl.multiple_of(i * tile, tile), tile)
+            return 0
+        lax.fori_loop(0, full, body, 0)
+        if width % tile:
+            gradient(r, full * tile, width % tile)
+        for d in range(n_dp - 1, 0, -1):
+            rs(r, d).start()
+
+    def d_c(r):
+        return remote(direction.at[r], dirs.at[mp, :, pl.ds(r * rc, rc)],
+                      dc_s.at[r], dc_r.at[r], to_core)
+
+    def d_x(r):
+        return remote(direction.at[r], dirs.at[mp, :, pl.ds(r * rc, rc)],
+                      dx_s.at[r], dx_r.at[r], to_x)
+
+    def d_f(r):
+        view = dirs.at[across, :, pl.ds(r * rc, rc)]
+        return remote(view, view, df_s.at[r], df_r.at[r], to_core)
+
+    def d_own(r):
+        return pltpu.make_async_copy(
+            direction.at[r], dirs.at[mp, :, pl.ds(r * rc, rc)], store_sem.at[4 + r])
+
+    def adam(r):
+        for d in range(1, n_dp):
+            rs(r, d).wait_recv()
+        cols = slice(r * rc, (r + 1) * rc)
+
+        def body(i, _):
+            at = pl.multiple_of(i * 16, 16)
+            own = pl.multiple_of(dp * hidden + i * 16, 16)
+            total = g_send[r, pl.ds(own, 16), :].astype(f32)
+            for d in range(n_dp - 1):
+                total = total + g_recv[d, r, pl.ds(at, 16), :].astype(f32)
+            first = beta_one * m_one[0, pl.ds(at, 16), cols] + (1.0 - beta_one) * total
+            second = beta_two * m_two[0, pl.ds(at, 16), cols] + (1.0 - beta_two) * total * total
+            m_one[0, pl.ds(at, 16), cols] = first
+            m_two[0, pl.ds(at, 16), cols] = second
+            direction[r, pl.ds(at, 16), :] = (
+                first / correction_one / (jnp.sqrt(second / correction_two) + epsilon)
+            ).astype(bf16)
+            return 0
+        lax.fori_loop(0, hidden // 16, body, 0)
+        d_x(r).start()
+        d_c(r).start()
+        d_own(r).start()
+
+    def forward(k):
+        w_x(k).wait_recv()
+        w_y(k).start()
+        w_f(k).start()
+
+    loads[3].wait()
+    loads[4].wait()
+    for k in range(WC // 2 + 1):
+        forward(k)
+    adam(0)
+    for k in range(WC // 2 + 1, WC):
+        forward(k)
+    for k in range(WC // 2):
+        w_y(k).wait_recv()
+        w_g(k).start()
+    adam(1)
+    st_one = pltpu.make_async_copy(m_one, first_out, store_sem.at[0])
+    st_two = pltpu.make_async_copy(m_two, second_out, store_sem.at[1])
+    st_one.start()
+    st_two.start()
+    b_x.wait_recv()
+    b_y.start()
+    b_f.start()
+    for k in range(WC // 2, WC):
+        w_y(k).wait_recv()
+        w_g(k).start()
+    b_y.wait_recv()
+    b_g.start()
+    for r in range(RC):
+        d_x(r).wait_recv()
+        d_f(r).start()
+
+    for r in range(RC):
+        pc(r).wait_send()
+        px(r).wait_send()
+        pf(r).wait_send()
+        for d in range(1, n_dp):
+            rs(r, d).wait_send()
+        d_x(r).wait_send()
+        d_c(r).wait()
+        d_own(r).wait()
+        d_f(r).wait()
+    for k in range(WC):
+        w_x(k).wait_send()
+        w_y(k).wait_send()
+        w_f(k).wait()
+        w_g(k).wait()
+    w_core.wait()
+    own_w.wait()
+    own_b.wait()
+    b_core.wait()
+    b_x.wait_send()
+    b_y.wait_send()
+    b_f.wait()
+    b_g.wait()
+    st_one.wait()
+    st_two.wait()
+
+
+def exchange(n_dp, tokens, out_grad, basis, weights, moment_one, moment_two):
+    tokens_own, depth = tokens.shape
+    width = out_grad.shape[1]
+    rank = basis.shape[1]
+    rc = rank // RC
+    hidden = weights.shape[1]
+    wide = weights.shape[2]
+    half = tokens_own // 2
+    dma = pltpu.SemaphoreType.DMA
+    any_spec = pl.BlockSpec(memory_space=pl.ANY)
+    pair = [dma((RC,)), dma((RC,))]
+    one = [dma((1,)), dma((1,))]
+    many = [dma((WC,)), dma((WC,))]
+    return pl.pallas_call(
+        functools.partial(exchange_kernel, n_dp),
+        name="exchange",
+        out_shape=(
+            jax.ShapeDtypeStruct(moment_one.shape, f32),
+            jax.ShapeDtypeStruct(moment_two.shape, f32),
+            jax.ShapeDtypeStruct((4, hidden, rank), bf16),
+            jax.ShapeDtypeStruct((4, depth, rank), bf16),
+            jax.ShapeDtypeStruct((4, hidden, wide), bf16),
+        ),
+        in_specs=[any_spec] * 6,
+        out_specs=(any_spec,) * 5,
+        scratch_shapes=[
+            pltpu.VMEM((tokens_own, depth), bf16),
+            pltpu.VMEM((depth, rank), bf16),
+            pltpu.VMEM((tokens_own, width), bf16),
+            pltpu.VMEM((half, rc), f32),
+            pltpu.VMEM((RC, half, rc), bf16),
+            pltpu.VMEM((RC, half, rc), bf16),
+            pltpu.VMEM((RC, half, rc), bf16),
+            pltpu.VMEM((RC, half, rc), bf16),
+            pltpu.VMEM((RC, tokens_own, rc), bf16),
+            pltpu.VMEM((RC, width, rc), bf16),
+            pltpu.VMEM((n_dp - 1, RC, hidden, rc), bf16),
+            pltpu.VMEM((1, hidden, rank), f32),
+            pltpu.VMEM((1, hidden, rank), f32),
+            pltpu.VMEM((RC, hidden, rc), bf16),
+            dma((5,)),
+            dma((4 + RC,)),
+            *pair, *pair, *pair,
+            dma((RC, n_dp - 1)), dma((RC, n_dp - 1)),
+            *pair, *pair, *pair,
+            *one, *one, *one, *one, *one,
+            *one, *many, *many, *many, *many,
+        ],
+        compiler_params=pltpu.CompilerParams(
+            collective_id=0, has_side_effects=True, vmem_limit_bytes=56 * 2**20
+        ),
+    )(tokens, out_grad, basis, weights, moment_one, moment_two)
+
+
+def update_kernel(weights, direction, basis, out):
+    delta = lax.dot_general(
+        direction[0], basis[0], (((1,), (1,)), ((), ())), preferred_element_type=f32
+    )
+    out[0] = (weights[0].astype(f32) - step_size * delta).astype(bf16)
+
+
+def update(walls, dirs, bases):
+    blocks, hidden, wide = walls.shape
+    parts, depth, rank = bases.shape
+    return pl.pallas_call(
+        update_kernel,
+        name="update",
+        grid=(blocks, parts),
+        out_shape=jax.ShapeDtypeStruct(walls.shape, bf16),
+        in_specs=[
+            pl.BlockSpec((1, hidden, depth), lambda i, j: (i, 0, j)),
+            pl.BlockSpec((1, hidden, rank), lambda i, j: (i, 0, 0)),
+            pl.BlockSpec((1, depth, rank), lambda i, j: (j, 0, 0)),
+        ],
+        out_specs=pl.BlockSpec((1, hidden, depth), lambda i, j: (i, 0, j)),
+        compiler_params=pltpu.CompilerParams(vmem_limit_bytes=40 * 2**20),
+    )(walls, dirs, bases)
+
+
+def shards_kernel(n_dp, tokens, out_grad, subspace_basis, weights, moment_first, moment_second):
+    first_new, second_new, dirs, bases, walls = exchange(
+        n_dp, tokens, out_grad, subspace_basis, weights, moment_first, moment_second)
+    return (update(walls, dirs, bases), first_new, second_new)
 
 
 def shards(tokens, out_grad, subspace_basis, weights, moment_first, moment_second):
@@ -40,8 +402,12 @@
 
 
 def solution(mesh):
+    if mesh.shape["mp"] == 4 and mesh.shape["grp"] == 2 and mesh.shape["dp"] == 4:
+        body = functools.partial(shards_kernel, mesh.shape["dp"])
+    else:
+        body = shards
     return jax.shard_map(
-        shards,
+        body,
         mesh=mesh,
         in_specs=(
             P(("grp", "dp"), "mp"),

time: 338 us -> 260 us (0.77)
  waiting for transfers between devices: 274 us -> 0 us
  Pallas kernels: 0 us -> 239 us
  matrix products: 24.7 us -> 0 us
  between operations: 13.8 us -> 0.65 us
    pallas_call x0 -> x2, Pallas kernels: none -> 239 us  [the longest x1 215 us: exchange(): pl.pallas_call(functools.partial(exchange_kernel, n_dp), name='exchange',...]
    all_gather x2 -> x0, waiting for transfers between devices: 173 us -> none  [the longest x1 140 us: shards(): result = lax.all_gather(updated[None], 'mp', axis=0, tiled=True)]
    reduce_scatter x1 -> x0, waiting for transfers between devices: 54.6 us -> none  [shards(): lax.psum_scatter(lax.dot_general(out_grad, projected, (((0,), (0,)), ((),...]
    psum x1 -> x0, waiting for transfers between devices: 45.6 us -> none  [shards(): projected = lax.psum(partial_value.astype(jnp.bfloat16), 'mp')]
    dot_general x3 -> x0, matrix products: 24.7 us -> none  [the longest x1 10.7 us: shards(): lax.dot_general(direction[0], lax.all_gather(subspace_basis, 'mp', axis=0...]
    unnamed x9 -> x11, local copies, waits for them, and re-layouts: 21.6 us -> 19 us
  transfers between devices with their start and end apart: 4 -> 0, of which waited for: 4 -> 0; matrix products, arithmetic and copies ran while one was open for 1% -> 0% of each run, Pallas kernels for 0% -> 0%
where the time goes in v1:
time: 260 us; the launch traced here: 259 us
  Pallas kernels  239 us (92%)
  local copies, waits for them, and re-layouts  19 us (7%)
    pallas_call x1, Pallas kernels, exchange(): pl.pallas_call(functools.partial(exchange_kernel, n_dp), name='exchange',...  215 us
    pallas_call x1, Pallas kernels, update(): pl.pallas_call(update_kernel, name='update', grid=(blocks, parts), out_sh...  24.8 us
    unnamed x11, local copies, waits for them, and re-layouts  19 us

profile of v1, /device:TPU:0, one launch (start us, length us, event | category | flops | bytes accessed | tf_op | source)
XLA Modules:
  0.0 259.1 jit_solution(11686282185066724202)
XLA Ops:
  0.6 12.1 %copy.9.out_grad = bf16[1536,2752]{1,0:T(8,128)(2,1)} copy(bf16[1536,2752]{0,1:T(8,128)(2,1)} %param.7) | data formatting | bytes 16908288 | tf_op args[1]
  12.7 214.7 %exchange.1 = (f32[1,688,512]{2,1,0:T(8,128)}, f32[1,688,512]{2,1,0:T(8,128)}, bf16[4,688,512]{2,1,0:T(8,128)(2,1)}, bf16[4,1024,512]{2,1,0:T(8,128)(2,1)}, bf16[4,688,4096]{2,1,0:T(8,128)(2,1)}) custom-call(bf16[1536,1024]{1,0:T(8,128)(2,1)} %tokens.1, bf16[1536,2752]{1,0:T(8,128)(2,1)} %copy.9.out_grad, bf16[1024,512]{1,0:T(8,128)(2,1)} %basis.1, ...), custom_call_target="tpu_custom_call" | custom-call | tf_op jit(solution)/shard_map/exchange/pallas_call | solution.py:304
  227.4 0.0 copy-start
  227.4 2.2 copy-done
  229.5 0.0 copy-start.1
  229.5 1.8 copy-done.1
  231.3 0.0 copy-start.3
  231.3 24.8 %update.1 = bf16[4,688,4096]{2,1,0:T(8,128)(2,1)} custom-call(bf16[4,688,4096]{2,1,0:T(8,128)(2,1)} %get-tuple-element.8.weights, bf16[4,688,512]{2,1,0:T(8,128)(2,1)S(1)} %copy-done.1, bf16[4,1024,512]{2,1,0:T(8,128)(2,1)S(1)} %copy-done), custom_call_target="tpu_custom_call" | custom-call | tf_op jit(solution)/shard_map/update/pallas_call | solution.py:355
  256.2 0.0 copy-done.3
  256.2 0.0 copy-start.2
  256.2 1.1 copy.12
  257.3 0.8 copy-done.2
  258.0 1.1 copy.13
Async XLA Ops:
  227.4 2.2 copy-start
  229.5 1.8 copy-start.1
  231.3 24.8 %copy-start.3 = (f32[1,688,512]{2,1,0:T(8,128)S(1)}, f32[1,688,512]{2,1,0:T(8,128)}, u32[]{:S(2)}) copy-start(f32[1,688,512]{2,1,0:T(8,128)} %get-tuple-element.17) | copy-start | bytes 4227076
  256.2 1.9 copy-start.2

commit v2 on v1

--- a/solution.py
+++ b/solution.py
@@ -20,19 +20,20 @@
 
 RC = 2
 WC = 8
+UC = 8
 
 
 def exchange_kernel(
     n_dp,
     tokens, out_grad, basis, weights, moment_one, moment_two,
     first_out, second_out, dirs, bases, walls,
-    tok_v, bas_v, og_v, p_own, p_send, p_recv, s_send, s_recv, proj,
-    g_send, g_recv, m_one, m_two, direction,
+    tok_v, bas_v, bas_t, og_v, p_own, p_send, p_recv, s_send, s_recv, proj,
+    g_send, g_recv, m_one, m_two, direction, w_v, bas_all,
     load_sem, store_sem,
     pc_s, pc_r, px_s, px_r, pf_s, pf_r, rs_s, rs_r,
     dc_s, dc_r, dx_s, dx_r, df_s, df_r,
     bc_s, bc_r, bx_s, bx_r, by_s, by_r, bf_s, bf_r, bg_s, bg_r,
-    wc_s, wc_r, wx_s, wx_r, wy_s, wy_r, wf_s, wf_r, wg_s, wg_r,
+    bz_s, bz_r, uo, uc_s, uc_r, wx_s, wx_r, wy_s, wy_r, wf_s, wf_r, wg_s, wg_r,
 ):
     grp = lax.axis_index("grp")
     dp = lax.axis_index("dp")
@@ -52,7 +53,8 @@
     wide = weights.shape[2]
     wh = wide // 2
     wc = wh // WC
-    bh = depth // 2
+    bh = rank // 2
+    bs = bh // n_dp
 
     def remote(src, dst, ss, rs, where):
         return pltpu.make_async_remote_copy(
@@ -64,7 +66,7 @@
         pltpu.make_async_copy(src, dst, load_sem.at[i])
         for i, (src, dst) in enumerate(
             [(tokens, tok_v), (basis, bas_v), (out_grad, og_v),
-             (moment_one, m_one), (moment_two, m_two)]
+             (moment_one, m_one), (moment_two, m_two), (weights.at[0], w_v)]
         )
     ]
     loads[1].start()
@@ -98,8 +100,6 @@
     def w_g(k):
         view = walls.at[across, :, w_cols(1 - grp, k)]
         return remote(view, view, wg_s.at[k], wg_r.at[k], to_core)
-
-    w_x(0).start()
 
     def project(r, row, dst):
         def body(i, _):
@@ -122,6 +122,33 @@
         return remote(view, view, pf_s.at[r], pf_r.at[r], to_core)
 
     loads[1].wait()
+    def turn(i, _):
+        at = pl.multiple_of(i * 128, 128)
+        bas_t[:, pl.ds(at, 128)] = bas_v[pl.ds(at, 128), :].T
+        return 0
+    lax.fori_loop(0, depth // 128, turn, 0)
+    own_b = pltpu.make_async_copy(bas_t, bases.at[mp], store_sem.at[2])
+    own_b.start()
+    b_core = remote(bas_t, bases.at[mp], bc_s.at[0], bc_r.at[0], to_core)
+    b_core.start()
+    rows_piece = pl.ds(grp * bh + dp * bs, bs)
+    rows_mine = pl.ds(grp * bh, bh)
+    rows_other = pl.ds((1 - grp) * bh, bh)
+    b_x = remote(bas_t.at[rows_piece, :], bases.at[mp, rows_piece, :],
+                 bx_s.at[0], bx_r.at[0], to_x)
+    b_x.start()
+    b_view_piece = bases.at[across, rows_piece, :]
+    b_z = [
+        remote(b_view_piece, b_view_piece, bz_s.at[d - 1], bz_r.at[d - 1],
+               {"dp": (dp + d) % n_dp})
+        for d in range(1, n_dp)
+    ]
+    b_view = bases.at[across, rows_mine, :]
+    b_y = remote(b_view, b_view, by_s.at[0], by_r.at[0], to_y)
+    b_f = remote(b_view, b_view, bf_s.at[0], bf_r.at[0], to_core)
+    b_view_other = bases.at[across, rows_other, :]
+    b_g = remote(b_view_other, b_view_other, bg_s.at[0], bg_r.at[0], to_core)
+
     loads[0].wait()
     for r in range(RC):
         project(r, (1 - core) * half, p_send.at[r])
@@ -130,48 +157,39 @@
         pc(r).wait_recv()
         s_send[r] = (p_own[...] + p_recv[r].astype(f32)).astype(bf16)
         px(r).start()
-
-    loads[3].start()
-    loads[4].start()
-
-    own_w = pltpu.make_async_copy(weights.at[0], walls.at[mp], store_sem.at[2])
-    own_w.start()
-    w_core = remote(weights.at[0], walls.at[mp], wc_s.at[0], wc_r.at[0], to_core)
-    w_core.start()
-    own_b = pltpu.make_async_copy(basis, bases.at[mp], store_sem.at[3])
-    own_b.start()
-    b_core = remote(basis, bases.at[mp], bc_s.at[0], bc_r.at[0], to_core)
-    b_core.start()
-    rows_mine = pl.ds(grp * bh, bh)
-    rows_other = pl.ds((1 - grp) * bh, bh)
-    b_x = remote(basis.at[rows_mine, :], bases.at[mp, rows_mine, :], bx_s.at[0], bx_r.at[0], to_x)
-    b_view = bases.at[across, rows_mine, :]
-    b_y = remote(b_view, b_view, by_s.at[0], by_r.at[0], to_y)
-    b_f = remote(b_view, b_view, bf_s.at[0], bf_r.at[0], to_core)
-    b_view_other = bases.at[across, rows_other, :]
-    b_g = remote(b_view_other, b_view_other, bg_s.at[0], bg_r.at[0], to_core)
+        w_x(r).start()
+        if r == 0:
+            b_x.wait_recv()
+            for copy in b_z:
+                copy.start()
+
+    for i in (3, 4, 5):
+        loads[i].start()
+
+    def forward(k):
+        w_x(k).wait_recv()
+        w_y(k).start()
+        w_f(k).start()
 
     def rs(r, d):
         to = (dp + d) % n_dp
         return remote(g_send.at[r, pl.ds(to * hidden, hidden), :], g_recv.at[d - 1, r],
                       rs_s.at[r, d - 1], rs_r.at[r, d - 1], {"dp": to})
 
-    width = out_grad.shape[1]
+    width = out_grad.shape[0]
     tile = 256
     full = width // tile
 
     def gradient(r, at, size):
-        g_send[r, pl.ds(at, size), :] = lax.dot_general(
-            og_v[:, pl.ds(at, size)], proj[r], (((0,), (0,)), ((), ())),
-            preferred_element_type=f32,
+        g_send[r, pl.ds(at, size), :] = jnp.dot(
+            og_v[pl.ds(at, size), :], proj[r], preferred_element_type=f32
         ).astype(bf16)
 
     for r in range(RC):
         px(r).wait_recv()
         if r == RC - 1:
-            for k in range(1, WC):
+            for k in range(RC, WC):
                 w_x(k).start()
-            b_x.start()
         proj[r, pl.ds(core * half, half), :] = (
             s_send[r].astype(f32) + s_recv[r].astype(f32)
         ).astype(bf16)
@@ -188,6 +206,12 @@
             gradient(r, full * tile, width % tile)
         for d in range(n_dp - 1, 0, -1):
             rs(r, d).start()
+        if r == 0:
+            forward(0)
+            for copy in b_z:
+                copy.wait_recv()
+            b_y.start()
+            b_f.start()
 
     def d_c(r):
         return remote(direction.at[r], dirs.at[mp, :, pl.ds(r * rc, rc)],
@@ -210,54 +234,84 @@
             rs(r, d).wait_recv()
         cols = slice(r * rc, (r + 1) * rc)
 
-        def body(i, _):
-            at = pl.multiple_of(i * 16, 16)
-            own = pl.multiple_of(dp * hidden + i * 16, 16)
-            total = g_send[r, pl.ds(own, 16), :].astype(f32)
+        for at in range(0, hidden, 128):
+            size = min(128, hidden - at)
+            rows = slice(at, at + size)
+            own = pl.multiple_of(dp * hidden + at, 16)
+            total = g_send[r, pl.ds(own, size), :].astype(f32)
             for d in range(n_dp - 1):
-                total = total + g_recv[d, r, pl.ds(at, 16), :].astype(f32)
-            first = beta_one * m_one[0, pl.ds(at, 16), cols] + (1.0 - beta_one) * total
-            second = beta_two * m_two[0, pl.ds(at, 16), cols] + (1.0 - beta_two) * total * total
-            m_one[0, pl.ds(at, 16), cols] = first
-            m_two[0, pl.ds(at, 16), cols] = second
-            direction[r, pl.ds(at, 16), :] = (
+                total = total + g_recv[d, r, rows, :].astype(f32)
+            first = beta_one * m_one[0, rows, cols] + (1.0 - beta_one) * total
+            second = beta_two * m_two[0, rows, cols] + (1.0 - beta_two) * total * total
+            m_one[0, rows, cols] = first
+            m_two[0, rows, cols] = second
+            direction[r, rows, :] = (
                 first / correction_one / (jnp.sqrt(second / correction_two) + epsilon)
             ).astype(bf16)
-            return 0
-        lax.fori_loop(0, hidden // 16, body, 0)
         d_x(r).start()
         d_c(r).start()
         d_own(r).start()
 
-    def forward(k):
-        w_x(k).wait_recv()
-        w_y(k).start()
-        w_f(k).start()
-
-    loads[3].wait()
-    loads[4].wait()
-    for k in range(WC // 2 + 1):
+    for i in (3, 4, 5):
+        loads[i].wait()
+    for k in range(1, WC // 2):
         forward(k)
+    b_y.wait_recv()
+    b_g.start()
     adam(0)
-    for k in range(WC // 2 + 1, WC):
+    for k in range(WC // 2, WC - 1):
         forward(k)
     for k in range(WC // 2):
         w_y(k).wait_recv()
         w_g(k).start()
+    b_core.wait_recv()
+    b_f.wait_recv()
+    b_g.wait_recv()
+    own_b.wait()
+    load_b = pltpu.make_async_copy(bases, bas_all, load_sem.at[6])
+    load_b.start()
+    forward(WC - 1)
     adam(1)
     st_one = pltpu.make_async_copy(m_one, first_out, store_sem.at[0])
     st_two = pltpu.make_async_copy(m_two, second_out, store_sem.at[1])
     st_one.start()
     st_two.start()
-    b_x.wait_recv()
-    b_y.start()
-    b_f.start()
-    for k in range(WC // 2, WC):
+    load_b.wait()
+
+    uw = wide // UC
+
+    def u_own(k):
+        return pltpu.make_async_copy(
+            w_v.at[:, pl.ds(k * uw, uw)], walls.at[mp, :, pl.ds(k * uw, uw)], uo.at[k])
+
+    def u_c(k):
+        return remote(w_v.at[:, pl.ds(k * uw, uw)], walls.at[mp, :, pl.ds(k * uw, uw)],
+                      uc_s.at[k], uc_r.at[k], to_core)
+
+    def u_step(k):
+        block, at = (k * uw) // depth, (k * uw) % depth
+        cols = slice(k * uw, (k + 1) * uw)
+        delta = jnp.dot(direction[0], bas_all[block, 0:rc, at:at + uw], preferred_element_type=f32)
+        for r in range(1, RC):
+            delta = delta + jnp.dot(
+                direction[r], bas_all[block, r * rc:(r + 1) * rc, at:at + uw],
+                preferred_element_type=f32)
+        w_v[:, cols] = (w_v[:, cols].astype(f32) - step_size * delta).astype(bf16)
+        u_own(k).start()
+        u_c(k).start()
+
+    for k in range(UC // 2):
+        u_step(k)
+    for k in range(WC // 2, WC - 1):
         w_y(k).wait_recv()
         w_g(k).start()
-    b_y.wait_recv()
-    b_g.start()
-    for r in range(RC):
+    d_x(0).wait_recv()
+    d_f(0).start()
+    for k in range(UC // 2, UC):
+        u_step(k)
+    w_y(WC - 1).wait_recv()
+    w_g(WC - 1).start()
+    for r in range(1, RC):
         d_x(r).wait_recv()
         d_f(r).start()
 
@@ -276,21 +330,23 @@
         w_y(k).wait_send()
         w_f(k).wait()
         w_g(k).wait()
-    w_core.wait()
-    own_w.wait()
-    own_b.wait()
-    b_core.wait()
+    for k in range(UC):
+        u_own(k).wait()
+        u_c(k).wait()
+    b_core.wait_send()
+    for copy in b_z:
+        copy.wait_send()
     b_x.wait_send()
     b_y.wait_send()
-    b_f.wait()
-    b_g.wait()
+    b_f.wait_send()
+    b_g.wait_send()
     st_one.wait()
     st_two.wait()
 
 
 def exchange(n_dp, tokens, out_grad, basis, weights, moment_one, moment_two):
     tokens_own, depth = tokens.shape
-    width = out_grad.shape[1]
+    width = out_grad.shape[0]
     rank = basis.shape[1]
     rc = rank // RC
     hidden = weights.shape[1]
@@ -308,7 +364,7 @@
             jax.ShapeDtypeStruct(moment_one.shape, f32),
             jax.ShapeDtypeStruct(moment_two.shape, f32),
             jax.ShapeDtypeStruct((4, hidden, rank), bf16),
-            jax.ShapeDtypeStruct((4, depth, rank), bf16),
+            jax.ShapeDtypeStruct((4, rank, depth), bf16),
             jax.ShapeDtypeStruct((4, hidden, wide), bf16),
         ),
         in_specs=[any_spec] * 6,
@@ -316,7 +372,8 @@
         scratch_shapes=[
             pltpu.VMEM((tokens_own, depth), bf16),
             pltpu.VMEM((depth, rank), bf16),
-            pltpu.VMEM((tokens_own, width), bf16),
+            pltpu.VMEM((rank, depth), bf16),
+            pltpu.VMEM((width, tokens_own), bf16),
             pltpu.VMEM((half, rc), f32),
             pltpu.VMEM((RC, half, rc), bf16),
             pltpu.VMEM((RC, half, rc), bf16),
@@ -328,49 +385,122 @@
             pltpu.VMEM((1, hidden, rank), f32),
             pltpu.VMEM((1, hidden, rank), f32),
             pltpu.VMEM((RC, hidden, rc), bf16),
-            dma((5,)),
+            pltpu.VMEM((hidden, wide), bf16),
+            pltpu.VMEM((4, rank, depth), bf16),
+            dma((7,)),
             dma((4 + RC,)),
             *pair, *pair, *pair,
             dma((RC, n_dp - 1)), dma((RC, n_dp - 1)),
             *pair, *pair, *pair,
             *one, *one, *one, *one, *one,
-            *one, *many, *many, *many, *many,
+            dma((n_dp - 1,)), dma((n_dp - 1,)), dma((UC,)), dma((UC,)), dma((UC,)),
+            *many, *many, *many, *many,
         ],
         compiler_params=pltpu.CompilerParams(
-            collective_id=0, has_side_effects=True, vmem_limit_bytes=56 * 2**20
+            collective_id=0, has_side_effects=True, vmem_limit_bytes=58 * 2**20
         ),
     )(tokens, out_grad, basis, weights, moment_one, moment_two)
 
 
-def update_kernel(weights, direction, basis, out):
-    delta = lax.dot_general(
-        direction[0], basis[0], (((1,), (1,)), ((), ())), preferred_element_type=f32
-    )
-    out[0] = (weights[0].astype(f32) - step_size * delta).astype(bf16)
-
-
-def update(walls, dirs, bases):
-    blocks, hidden, wide = walls.shape
-    parts, depth, rank = bases.shape
+def update_kernel(
+    walls, dirs, bases, first, second, out, first_out, second_out,
+    w_v, d_v, b_v, m_v, d_sem, b_sem, m_in, m_out, w_in, w_out,
+):
+    base = 2 * (lax.axis_index("mp") // 2)
+    hidden, wide = walls.shape[1:]
+    parts, _, depth = bases.shape
+    where = (2 - base, 3 - base, base, base + 1)
+    cuts = [hidden * i // parts // 16 * 16 for i in range(parts)] + [hidden]
+
+    def piece(slot, p):
+        if slot < 2:
+            return (slice(None), pl.ds(p * depth, depth))
+        return (pl.ds(cuts[p], cuts[p + 1] - cuts[p]), slice(None))
+
+    def fetch(slot, p):
+        at = piece(slot, p)
+        return pltpu.make_async_copy(
+            walls.at[(where[slot],) + at], w_v.at[(slot,) + at], w_in.at[slot, p])
+
+    def put(slot, p):
+        at = piece(slot, p)
+        return pltpu.make_async_copy(
+            w_v.at[(slot,) + at], out.at[(where[slot],) + at], w_out.at[slot, p])
+
+    fetch_d = [pltpu.make_async_copy(dirs.at[where[i]], d_v.at[i], d_sem.at[i]) for i in range(2)]
+    fetch_b = [pltpu.make_async_copy(bases.at[p], b_v.at[p], b_sem.at[p]) for p in range(parts)]
+    fetch_m = [pltpu.make_async_copy(first, m_v.at[0], m_in.at[0]),
+               pltpu.make_async_copy(second, m_v.at[1], m_in.at[1])]
+    put_m = [pltpu.make_async_copy(m_v.at[0], first_out, m_out.at[0]),
+             pltpu.make_async_copy(m_v.at[1], second_out, m_out.at[1])]
+    fetch_d[0].start()
+    for p in range(parts):
+        fetch_b[p].start()
+        fetch(0, p).start()
+        fetch(2, p).start()
+    fetch_d[1].start()
+    for p in range(parts):
+        fetch(1, p).start()
+        fetch(3, p).start()
+    for copy in fetch_m:
+        copy.start()
+
+    for slot in range(2):
+        fetch_d[slot].wait()
+        for p in range(parts):
+            if slot == 0:
+                fetch_b[p].wait()
+            fetch(slot, p).wait()
+            for at in range(0, depth, 512):
+                cols = slice(p * depth + at, p * depth + at + 512)
+                delta = jnp.dot(d_v[slot], b_v[p, :, at:at + 512], preferred_element_type=f32)
+                w_v[slot, :, cols] = (
+                    w_v[slot, :, cols].astype(f32) - step_size * delta
+                ).astype(bf16)
+            put(slot, p).start()
+            fetch(slot + 2, p).wait()
+            put(slot + 2, p).start()
+    for copy_in, copy in zip(fetch_m, put_m):
+        copy_in.wait()
+        copy.start()
+    for slot in range(4):
+        for p in range(parts):
+            put(slot, p).wait()
+    for copy in put_m:
+        copy.wait()
+
+
+def update(walls, dirs, bases, first, second):
+    parts, rank, depth = bases.shape
+    hidden = walls.shape[1]
+    any_spec = pl.BlockSpec(memory_space=pl.ANY)
+    dma = pltpu.SemaphoreType.DMA
     return pl.pallas_call(
         update_kernel,
         name="update",
-        grid=(blocks, parts),
-        out_shape=jax.ShapeDtypeStruct(walls.shape, bf16),
-        in_specs=[
-            pl.BlockSpec((1, hidden, depth), lambda i, j: (i, 0, j)),
-            pl.BlockSpec((1, hidden, rank), lambda i, j: (i, 0, 0)),
-            pl.BlockSpec((1, depth, rank), lambda i, j: (j, 0, 0)),
+        out_shape=(
+            jax.ShapeDtypeStruct(walls.shape, bf16),
+            jax.ShapeDtypeStruct(first.shape, f32),
+            jax.ShapeDtypeStruct(second.shape, f32),
+        ),
+        in_specs=[any_spec] * 5,
+        out_specs=(any_spec,) * 3,
+        scratch_shapes=[
+            pltpu.VMEM(walls.shape, bf16),
+            pltpu.VMEM((2, hidden, rank), bf16),
+            pltpu.VMEM(bases.shape, bf16),
+            pltpu.VMEM((2,) + first.shape, f32),
+            dma((2,)), dma((parts,)), dma((2,)), dma((2,)),
+            dma((4, parts)), dma((4, parts)),
         ],
-        out_specs=pl.BlockSpec((1, hidden, depth), lambda i, j: (i, 0, j)),
-        compiler_params=pltpu.CompilerParams(vmem_limit_bytes=40 * 2**20),
-    )(walls, dirs, bases)
+        compiler_params=pltpu.CompilerParams(vmem_limit_bytes=60 * 2**20),
+    )(walls, dirs, bases, first, second)
 
 
 def shards_kernel(n_dp, tokens, out_grad, subspace_basis, weights, moment_first, moment_second):
     first_new, second_new, dirs, bases, walls = exchange(
-        n_dp, tokens, out_grad, subspace_basis, weights, moment_first, moment_second)
-    return (update(walls, dirs, bases), first_new, second_new)
+        n_dp, tokens, out_grad.T, subspace_basis, weights, moment_first, moment_second)
+    return update(walls, dirs, bases, first_new, second_new)
 
 
 def shards(tokens, out_grad, subspace_basis, weights, moment_first, moment_second):

time: 260 us -> 125 us (0.48)
  Pallas kernels: 239 us -> 124 us
  local copies, waits for them, and re-layouts: 19 us -> 0 us
    pallas_call x1, Pallas kernels: 215 us -> 107 us  [exchange(): pl.pallas_call(functools.partial(exchange_kernel, n_dp), name='exchange',...]
    unnamed x11 -> x0, local copies, waits for them, and re-layouts: 19 us -> none
    pallas_call x1, Pallas kernels: 24.8 us -> 17.4 us  [update(): pl.pallas_call(update_kernel, name='update', out_shape=(jax.ShapeDtypeStr...]
where the time goes in v2:
time: 125 us
  Pallas kernels  124 us (99%)
    pallas_call x1, Pallas kernels, exchange(): pl.pallas_call(functools.partial(exchange_kernel, n_dp), name='exchange',...  107 us
    pallas_call x1, Pallas kernels, update(): pl.pallas_call(update_kernel, name='update', out_shape=(jax.ShapeDtypeStr...  17.4 us

profile of v2, /device:TPU:0, one launch (start us, length us, event | category | flops | bytes accessed | tf_op | source)
XLA Modules:
  0.0 124.6 jit_solution(8933115160381544560)
XLA Ops:
  0.6 106.5 %exchange.1 = (f32[1,688,512]{2,1,0:T(8,128)}, f32[1,688,512]{2,1,0:T(8,128)}, bf16[4,688,512]{2,1,0:T(8,128)(2,1)}, bf16[4,512,1024]{2,1,0:T(8,128)(2,1)}, bf16[4,688,4096]{2,1,0:T(8,128)(2,1)}) custom-call(bf16[1536,1024]{1,0:T(8,128)(2,1)} %tokens.1, bf16[2752,1536]{1,0:T(8,128)(2,1)} %bitcast.1, bf16[1024,512]{1,0:T(8,128)(2,1)} %basis.1, ...), custom_call_target="tpu_custom_call" | custom-call | tf_op jit(solution)/shard_map/exchange/pallas_call | solution.py:360
  107.2 17.4 %update.1 = (bf16[4,688,4096]{2,1,0:T(8,128)(2,1)}, f32[1,688,512]{2,1,0:T(8,128)}, f32[1,688,512]{2,1,0:T(8,128)}) custom-call(bf16[4,688,4096]{2,1,0:T(8,128)(2,1)} %get-tuple-element.8.walls, bf16[4,688,512]{2,1,0:T(8,128)(2,1)} %get-tuple-element.9.dirs, bf16[4,512,1024]{2,1,0:T(8,128)(2,1)} %get-tuple-element.10.bases, ...), custom_call_target="tpu_custom_call" | custom-call | tf_op jit(solution)/shard_map/update/pallas_call | solution.py:478
